TPU v7x, 256 devices: a whole 4x4x8 slice. The times are simulated.
256 devices in a mesh: rows: 4 (over y), cols: 64 (over x, z, core).
Axes of the slice: x: 4, y: 4, z: 8, core: 2. Of those that a mesh axis runs over, the one named last changes fastest.
Arguments:
- sensitivity: bfloat16 [4, 256, 512, 512], P('rows', 'cols'), may hold values from -0.25 to 0.25
- tile_rows: int32 [4, 256], P('rows', 'cols'), may hold values from 0 to 127, as said below
- tile_cols: int32 [4, 256], P('rows', 'cols'), may hold values from 0 to 1, as said below
- kept_counts: int32 [4, 256], P('rows', 'cols'), may hold values from 0 to 512, as said below
- misfit: float32 [262144], P('rows'), may hold values from -6 to 6
- data_weight: float32 [262144], P('rows'), may hold values from 0.3 to 3
- depth_weight: float32 [65536], P('cols'), may hold values from 0.25 to 3
- density: float32 [65536], P('cols'), may hold values from -6 to 6
Outputs:
- new_density: float32 [65536], P('cols')
- new_misfit: float32 [262144], P(('rows', 'cols'))
Inputs may be any that keep to these rules, and one draw needn't show every extreme that they name: Within the 4 slots of one device the pairs (tile_rows, tile_cols) are distinct. Within the 4 slots of one device the pairs (tile_rows, tile_cols) are distinct. A slot with kept_counts 0 is empty, and empty slots come after all live slots of a device; a live slot keeps 512 // 2 or more coefficients; every device has a live slot, and some device has all 4 slots live.
All inputs are finite; a program needn't handle non-finite values.
Results may differ from a plain program's by a relative error of at most 0.033.
Values may be sent and summed in bfloat16 or wider, within the bound.
No kernel may reach another device: no remote copies, remote signals or barrier semaphores. Data moves between devices by JAX's collectives and lax.ppermute only.
A program may use at most 64 MiB of HBM per device.

v0:
```python
import math
import jax
import jax.numpy as jnp
from jax import lax
from jax.sharding import PartitionSpec as P

ITERS = 4
damping = 1.0


def haar_matrix(tile_size):
    rows_index = jnp.arange(tile_size, dtype=jnp.int32)[:, None]
    column_index = jnp.arange(tile_size, dtype=jnp.int32)[None, :]
    levels = jnp.zeros_like(rows_index)
    for bit_shift in range(1, tile_size.bit_length()):
        levels = levels + (rows_index >= 1 << bit_shift).astype(jnp.int32)
    support = jnp.right_shift(tile_size, levels)
    offset = (rows_index - jnp.left_shift(1, levels)) * support
    inside = (column_index >= offset) & (column_index < offset + support)
    polarity = jnp.where(column_index < offset + support // 2, 1.0, -1.0)
    detail = jnp.where(inside, polarity, 0.0) / jnp.sqrt(support.astype(jnp.float32))
    coarse = jnp.full((1, tile_size), 1.0 / math.sqrt(tile_size), jnp.float32)
    return jnp.concatenate([coarse, detail[1:]], axis=0)


def squared_norm(values):
    return lax.psum(jnp.sum(values * values), "cols")


def per_device(
    sensitivity, tile_rows, tile_cols, kept_counts, misfit, data_weight, depth_weight, density
):
    tile_stack = sensitivity[0]
    slot_rows = tile_rows[0]
    slot_cols = tile_cols[0]
    slot_kept = kept_counts[0]
    tile_size = tile_stack.shape[-1]
    data_blocks = misfit.shape[0] // tile_size
    model_blocks = density.shape[0] // tile_size
    wavelet = haar_matrix(tile_size)
    coefficient_index = jnp.arange(tile_size, dtype=jnp.int32)
    live_mask = coefficient_index[None, :] < slot_kept[:, None]
    pick_rows = slot_rows[:, None] == jnp.arange(data_blocks, dtype=jnp.int32)[None, :]
    pick_cols = slot_cols[:, None] == jnp.arange(model_blocks, dtype=jnp.int32)[None, :]
    share_len = misfit.shape[0] // lax.axis_size("cols")
    share_start = lax.axis_index("cols") * share_len
    squared = data_weight * data_weight

    def adjoint_part(weighted):
        data_rows = weighted.reshape(data_blocks, tile_size)
        picked = jnp.dot(
            pick_rows.astype(jnp.bfloat16), data_rows, preferred_element_type=jnp.float32
        ).astype(jnp.bfloat16)
        products = jnp.einsum("sab,sa->sb", tile_stack, picked, preferred_element_type=jnp.float32)
        products = jnp.where(live_mask, products, 0.0)
        block_sums = jnp.dot(
            pick_cols.T.astype(jnp.float32), products, precision=lax.Precision.HIGHEST
        )
        cell_part = jnp.dot(block_sums, wavelet, precision=lax.Precision.HIGHEST).reshape(-1)
        return lax.psum(cell_part, "rows")

    rhs = depth_weight * adjoint_part((squared * misfit).astype(jnp.bfloat16)) - damping * density
    solution = jnp.zeros_like(density)
    residual = rhs
    direction = rhs
    norm_now = squared_norm(residual)
    change = jnp.zeros_like(misfit)
    for iteration in range(ITERS):
        coeffs = jnp.dot(
            (depth_weight * direction).reshape(model_blocks, tile_size),
            wavelet.T,
            precision=lax.Precision.HIGHEST,
        )
        forward_picked = jnp.dot(
            pick_cols.astype(jnp.float32), coeffs, precision=lax.Precision.HIGHEST
        )
        forward_picked = jnp.where(live_mask, forward_picked, 0.0).astype(jnp.bfloat16)
        forward_products = jnp.einsum(
            "sab,sb->sa", tile_stack, forward_picked, preferred_element_type=jnp.float32
        )
        summed = jnp.dot(
            pick_rows.T.astype(jnp.float32), forward_products, precision=lax.Precision.HIGHEST
        )
        partial_data = summed.reshape(-1)
        image_data = lax.psum(partial_data, "cols")
        weighted = (squared * image_data).astype(jnp.bfloat16)
        image_cells = depth_weight * adjoint_part(weighted) + damping * direction
        curvature_sum = lax.psum(jnp.sum(direction * image_cells), "cols")
        step_length = norm_now / curvature_sum
        solution = solution + step_length * direction
        residual = residual - step_length * image_cells
        change = change + step_length * image_data
        if iteration + 1 < ITERS:
            norm_next = squared_norm(residual)
            direction = residual + norm_next / norm_now * direction
            norm_now = norm_next
    new_density = density + depth_weight * solution
    new_misfit = lax.dynamic_slice_in_dim(misfit - change, share_start, share_len)
    return (new_density, new_misfit)


def solution(mesh):
    return jax.shard_map(
        per_device,
        mesh=mesh,
        in_specs=(
            P("rows", "cols", None, None),
            P("rows", "cols"),
            P("rows", "cols"),
            P("rows", "cols"),
            P("rows"),
            P("rows"),
            P("cols"),
            P("cols"),
        ),
        out_specs=(P("cols"), P(("rows", "cols"))),
        check_vma=False,
    )
```

profile of v0, /device:TPU:1, one launch (start us, length us, event | category | flops | bytes accessed | tf_op | source)
XLA Modules:
  0.0 1661.8 jit_solution(10881890196141592567)
XLA Ops:
  7.3 1.2 multiply_convert_fusion.4
  8.9 0.8 fusion.22
  9.7 0.4 fusion.16
  10.8 0.7 convolution_bitcast_fusion.8
  11.4 9.5 psum.119
  21.0 0.9 fusion.42
  22.2 0.6 fusion.14
  22.8 0.4 convolution_bitcast_fusion.3
  23.2 0.8 copy.29
  24.1 178.2 %all-reduce.7.cloned.1.call-done = f32[65536]{0:T(1024)} async-done(((f32[65536]{0:T(1024)}), f32[65536]{0:T(1024)}) %all-reduce.7.cloned.1.call-update) | async-done | bytes 262160 | tf_op jit(solution)/shard_map/psum | solution.py:85
  202.3 1.0 multiply_convert_fusion.3
  203.3 0.7 reshape.190
  204.0 1.1 fusion.23
  205.1 0.4 fusion.12
  205.5 0.9 fusion.51
  206.4 0.7 convolution_bitcast_fusion.7
  207.1 8.4 psum.122
  215.6 0.6 multiply_reduce_fusion.5
  216.2 125.2 %all-reduce.1 = (f32[]{:T(128)}, f32[]{:T(128)}) all-reduce(f32[]{:T(128)} %get-tuple-element.3, f32[]{:T(128)} %get-tuple-element.2), channel_id=1, replica_groups=mesh['rows'=4,'cols'=64] {'cols'}, use_global_device_ids=true, to_apply=%region_2.3 | all-reduce | flops 2 | bytes 16 | tf_op jit(solution)/shard_map/psum | solution.py:27
  342.7 0.6 multiply_reduce_fusion.4
  343.3 124.8 %psum.124 = f32[]{:T(128)} all-reduce(f32[]{:T(128)} %multiply_reduce_fusion.4), channel_id=1, replica_groups=mesh['rows'=4,'cols'=64] {'cols'}, use_global_device_ids=true, to_apply=%region_8.9 | all-reduce | flops 1 | bytes 8 | tf_op jit(solution)/shard_map/psum | solution.py:27
  469.5 0.9 fusion.39
  470.6 0.6 fusion.10
  471.3 0.4 convolution_bitcast_fusion.2
  471.7 0.8 copy.31
  472.5 167.1 %all-reduce.9.cloned.1.call-done = f32[65536]{0:T(1024)} async-done(((f32[65536]{0:T(1024)}), f32[65536]{0:T(1024)}) %all-reduce.9.cloned.1.call-update) | async-done | bytes 262160 | tf_op jit(solution)/shard_map/psum | solution.py:85
  639.6 1.0 multiply_convert_fusion.2
  640.6 0.7 reshape.194
  641.4 1.1 fusion.24
  642.8 0.9 fusion.49
  643.8 0.7 convolution_bitcast_fusion.6
  644.5 8.4 psum.126
  652.9 0.6 multiply_reduce_fusion.3
  653.5 125.2 %psum.127 = f32[]{:T(128)} all-reduce(f32[]{:T(128)} %multiply_reduce_fusion.3), channel_id=1, replica_groups=mesh['rows'=4,'cols'=64] {'cols'}, use_global_device_ids=true, to_apply=%region_12.13 | all-reduce | flops 1 | bytes 8 | tf_op jit(solution)/shard_map/psum | solution.py:88
  780.0 0.6 multiply_reduce_fusion.2
  780.6 124.8 %psum.128 = f32[]{:T(128)} all-reduce(f32[]{:T(128)} %get-tuple-element.8), channel_id=1, replica_groups=mesh['rows'=4,'cols'=64] {'cols'}, use_global_device_ids=true, to_apply=%region_14.15 | all-reduce | flops 1 | bytes 8 | tf_op jit(solution)/shard_map/psum | solution.py:27
  906.8 0.9 fusion.36
  908.0 0.6 fusion.6
  908.6 0.4 convolution_bitcast_fusion.1
  909.1 0.8 copy.33
  909.9 167.0 %all-reduce.11.cloned.1.call-done = f32[65536]{0:T(1024)} async-done(((f32[65536]{0:T(1024)}), f32[65536]{0:T(1024)}) %all-reduce.11.cloned.1.call-update) | async-done | bytes 262160 | tf_op jit(solution)/shard_map/psum | solution.py:85
  1076.9 1.0 multiply_convert_fusion.1
  1077.9 0.7 reshape.198
  1078.7 1.1 fusion.25
  1080.5 0.7 convolution_bitcast_fusion.5
  1081.2 8.4 psum.130
  1089.6 0.7 multiply_reduce_fusion.1
  1090.3 125.1 %psum.131 = f32[]{:T(128)} all-reduce(f32[]{:T(128)} %multiply_reduce_fusion.1), channel_id=1, replica_groups=mesh['rows'=4,'cols'=64] {'cols'}, use_global_device_ids=true, to_apply=%region_18.19 | all-reduce | flops 1 | bytes 8 | tf_op jit(solution)/shard_map/psum | solution.py:88
  1216.8 0.6 multiply_reduce_fusion
  1217.4 124.6 %psum.132 = f32[]{:T(128)} all-reduce(f32[]{:T(128)} %multiply_reduce_fusion), channel_id=1, replica_groups=mesh['rows'=4,'cols'=64] {'cols'}, use_global_device_ids=true, to_apply=%region_20.21 | all-reduce | flops 1 | bytes 8 | tf_op jit(solution)/shard_map/psum | solution.py:27
  1343.4 0.9 fusion.33
  1344.6 0.6 fusion.2
  1345.2 0.4 convolution_bitcast_fusion
  1345.7 0.8 copy.35
  1346.5 167.2 %all-reduce.13.cloned.1.call-done = f32[65536]{0:T(1024)} async-done(((f32[65536]{0:T(1024)}), f32[65536]{0:T(1024)}) %all-reduce.13.cloned.1.call-update) | async-done | bytes 262160 | tf_op jit(solution)/shard_map/psum | solution.py:85
  1513.6 1.0 multiply_convert_fusion
  1514.7 0.8 fusion.26
  1515.6 0.4 fusion
  1515.9 0.9 fusion.45
  1516.9 0.7 convolution_bitcast_fusion.4
  1517.6 8.4 psum.134
  1526.0 1.4 fusion.72
  1527.4 125.2 %psum.135 = f32[]{:T(128)} all-reduce(f32[]{:T(128)} %fusion.72), channel_id=1, replica_groups=mesh['rows'=4,'cols'=64] {'cols'}, use_global_device_ids=true, to_apply=%region_24.25 | all-reduce | flops 1 | bytes 8 | tf_op jit(solution)/shard_map/psum | solution.py:88
  1653.9 1.4 dynamic-slice_subtract_fusion
  (76 shorter events, 3.4 us)
Async XLA Ops:
  7.2 2.6 copy-start
  7.2 2.9 copy-start.14
  7.2 2.9 copy-start.10
  7.2 195.1 %all-reduce.7.cloned.1.call-start = ((), (), s32[]{:S(2)}) async-start(), calls=%async_computation | async-start | bytes 524288 | tf_op jit(solution)/shard_map/psum | solution.py:85
  9.7 11.3 copy-start.2
  9.7 11.3 copy-start.6
  10.8 12.1 copy-start.7
  21.0 181.3 %copy-start.1 = (f32[65536]{0:T(1024)S(1)}, f32[65536]{0:T(1024)}, u32[]{:S(2)}) copy-start(f32[65536]{0:T(1024)} %param.13) | copy-start | bytes 786436
  24.0 615.6 %all-reduce.9.cloned.1.call-start = ((), (), s32[]{:S(2)}) async-start(), calls=%async_computation.1 | async-start | bytes 524288 | tf_op jit(solution)/shard_map/psum | solution.py:85
  205.1 265.3 %copy-start.11 = (s32[1,4]{1,0:T(1,128)S(1)}, s32[1,4]{1,0:T(1,128)}, u32[]{:S(2)}) copy-start(s32[1,4]{1,0:T(1,128)} %param.11) | copy-start | bytes 52
  205.1 265.3 %copy-start.15 = (s32[1,4]{1,0:T(1,128)S(1)}, s32[1,4]{1,0:T(1,128)}, u32[]{:S(2)}) copy-start(s32[1,4]{1,0:T(1,128)} %param.10) | copy-start | bytes 52
  472.5 604.5 %all-reduce.11.cloned.1.call-start = ((), (), s32[]{:S(2)}) async-start(), calls=%async_computation.2 | async-start | bytes 524288 | tf_op jit(solution)/shard_map/psum | solution.py:85
  642.4 265.3 %copy-start.12 = (s32[1,4]{1,0:T(1,128)S(1)}, s32[1,4]{1,0:T(1,128)}, u32[]{:S(2)}) copy-start(s32[1,4]{1,0:T(1,128)} %param.11) | copy-start | bytes 52
  642.5 265.3 %copy-start.16 = (s32[1,4]{1,0:T(1,128)S(1)}, s32[1,4]{1,0:T(1,128)}, u32[]{:S(2)}) copy-start(s32[1,4]{1,0:T(1,128)} %param.10) | copy-start | bytes 52
  643.8 264.9 %copy-start.8 = (s32[1,4]{1,0:T(1,128)S(1)}, s32[1,4]{1,0:T(1,128)}, u32[]{:S(2)}) copy-start(s32[1,4]{1,0:T(1,128)} %param.9) | copy-start | bytes 52
  780.6 129.2 %copy-start.3 = (f32[1024]{0:T(1024)}, f32[1024]{0:T(1024)S(1)}, u32[]{:S(2)}) copy-start(f32[1024]{0:T(1024)S(1)} %get-tuple-element.9) | copy-start | bytes 12292
  909.9 603.8 %all-reduce.13.cloned.1.call-start = ((), (), s32[]{:S(2)}) async-start(), calls=%async_computation.3 | async-start | bytes 524288 | tf_op jit(solution)/shard_map/psum | solution.py:85
  1078.7 1.5 copy-start.13
  1078.7 1.5 copy-start.17
  1078.7 138.1 %copy-start.4 = (f32[1024]{0:T(1024)S(1)}, f32[1024]{0:T(1024)}, u32[]{:S(2)}) copy-start(f32[1024]{0:T(1024)} %copy-done.3) | copy-start | bytes 12292
  1080.5 264.8 %copy-start.9 = (s32[1,4]{1,0:T(1,128)S(1)}, s32[1,4]{1,0:T(1,128)}, u32[]{:S(2)}) copy-start(s32[1,4]{1,0:T(1,128)} %param.9) | copy-start | bytes 52
  1089.6 256.9 %copy-start.5 = (f32[1024]{0:T(1024)}, f32[1024]{0:T(1024)S(1)}, u32[]{:S(2)}) copy-start(f32[1024]{0:T(1024)S(1)} %psum.130) | copy-start | bytes 12292
Sparse Core Ops, SparseCore 0:
  24.2 178.0 all-reduce.6
  472.6 166.9 all-reduce.8
  910.0 166.9 all-reduce.10
  1346.6 167.0 all-reduce.12
where the time goes:
time: 1660 us
  blocking collectives  918 us (55%)
  waiting for transfers between devices  680 us (41%)
  between operations  23.4 us (1%)
  matrix products  22.4 us (1%)
    psum x4, waiting for transfers between devices, per_device(): image_data = lax.psum(partial_data, 'cols')  679 us
    psum x4, blocking collectives, squared_norm(): return lax.psum(jnp.sum(values * values), 'cols')  499 us
    psum x3, blocking collectives, per_device(): curvature_sum = lax.psum(jnp.sum(direction * image_cells), 'cols')  376 us
    psum x5, blocking collectives, adjoint_part(): return lax.psum(cell_part, 'rows')  43.3 us
  transfers between devices with their start and end apart: 4, of which 4 were waited for; matrix products, arithmetic and copies ran while one was open for 0% of the time, Pallas kernels for 0%

commit v1 on v0

--- a/solution.py
+++ b/solution.py
@@ -82,7 +82,7 @@
             pick_rows.T.astype(jnp.float32), forward_products, precision=lax.Precision.HIGHEST
         )
         partial_data = summed.reshape(-1)
-        image_data = lax.psum(partial_data, "cols")
+        image_data = jnp.sum(lax.all_gather(partial_data, "cols"), axis=0)
         weighted = (squared * image_data).astype(jnp.bfloat16)
         image_cells = depth_weight * adjoint_part(weighted) + damping * direction
         curvature_sum = lax.psum(jnp.sum(direction * image_cells), "cols")

time: 1660 us -> 1420 us (0.86)
  waiting for transfers between devices: 680 us -> 378 us
  other arithmetic: 12.1 us -> 59.3 us
    psum x4 -> x0, waiting for transfers between devices: 679 us -> none  [per_device(): image_data = lax.psum(partial_data, 'cols')]
    all_gather x0 -> x4, waiting for transfers between devices: none -> 378 us  [per_device(): image_data = jnp.sum(lax.all_gather(partial_data, 'cols'), axis=0)]
    reduce_sum x0 -> x4, other arithmetic: none -> 48 us  [per_device(): image_data = jnp.sum(lax.all_gather(partial_data, 'cols'), axis=0)]
where the time goes in v1:
time: 1420 us
  blocking collectives  922 us (65%)
  waiting for transfers between devices  378 us (27%)
  other arithmetic  59.3 us (4%)
  matrix products  23.8 us (2%)
  between operations  22.7 us (2%)
    psum x4, blocking collectives, squared_norm(): return lax.psum(jnp.sum(values * values), 'cols')  500 us
    psum x3, blocking collectives, per_device(): curvature_sum = lax.psum(jnp.sum(direction * image_cells), 'cols')  379 us
    all_gather x4, waiting for transfers between devices, per_device(): image_data = jnp.sum(lax.all_gather(partial_data, 'cols'), axis=0)  378 us
    reduce_sum x4, other arithmetic, per_device(): image_data = jnp.sum(lax.all_gather(partial_data, 'cols'), axis=0)  48 us
    psum x5, blocking collectives, adjoint_part(): return lax.psum(cell_part, 'rows')  43.3 us
  transfers between devices with their start and end apart: 4, of which 4 were waited for; matrix products, arithmetic and copies ran while one was open for 0% of the time, Pallas kernels for 0%

profile of v1, /device:TPU:1, one launch (start us, length us, event | category | flops | bytes accessed | tf_op | source)
XLA Modules:
  0.0 1416.2 jit_solution(4283489816546856888)
XLA Ops:
  7.3 1.2 multiply_convert_fusion.4
  8.9 0.8 fusion.22
  10.8 0.7 convolution_bitcast_fusion.4
  11.4 9.5 psum.91
  21.0 0.9 fusion.42
  22.2 0.6 fusion.14
  22.8 0.4 fusion.55
  23.2 1.0 reshape.188
  24.3 102.8 %all-gather.9.cloned.1.call-done = f32[64,1,65536]{2,1,0:T(1,128)} async-done(((f32[1,1,65536]{2,1,0:T(1,128)}), f32[64,1,65536]{2,1,0:T(1,128)}) %all-gather.9.cloned.1.call-update) | async-done | bytes 16777232 | tf_op jit(solution)/shard_map/all_gather | solution.py:85
  127.2 12.0 reduce_sum.109
  139.2 1.0 multiply_convert_fusion.3
  140.1 0.7 reshape.177
  140.9 1.1 fusion.23
  142.3 0.9 fusion.54
  143.3 0.7 convolution_bitcast_fusion.3
  144.0 8.4 psum.93
  152.4 0.6 multiply_reduce_fusion.5
  153.0 126.3 %all-reduce.1 = (f32[]{:T(128)}, f32[]{:T(128)}) all-reduce(f32[]{:T(128)} %get-tuple-element.3, f32[]{:T(128)} %get-tuple-element.2), channel_id=1, replica_groups=mesh['rows'=4,'cols'=64] {'cols'}, use_global_device_ids=true, to_apply=%region_2.3 | all-reduce | flops 2 | bytes 16 | tf_op jit(solution)/shard_map/psum | solution.py:27
  280.6 0.6 multiply_reduce_fusion.4
  281.2 124.7 %psum.95 = f32[]{:T(128)} all-reduce(f32[]{:T(128)} %multiply_reduce_fusion.4), channel_id=1, replica_groups=mesh['rows'=4,'cols'=64] {'cols'}, use_global_device_ids=true, to_apply=%region_8.9 | all-reduce | flops 1 | bytes 8 | tf_op jit(solution)/shard_map/psum | solution.py:27
  407.2 0.9 fusion.39
  408.3 0.6 fusion.10
  409.0 1.1 fusion.52
  410.1 2.0 reshape.190
  412.1 91.7 %all-gather.11.cloned.1.call-done = f32[64,1,65536]{2,1,0:T(1,128)} async-done(((f32[1,1,65536]{2,1,0:T(1,128)}), f32[64,1,65536]{2,1,0:T(1,128)}) %all-gather.11.cloned.1.call-update) | async-done | bytes 16777232 | tf_op jit(solution)/shard_map/all_gather | solution.py:85
  503.8 12.0 reduce_sum.112
  515.8 1.0 multiply_convert_fusion.2
  516.8 0.7 reshape.180
  517.5 1.1 fusion.24
  519.0 0.9 fusion.51
  520.0 0.7 convolution_bitcast_fusion.2
  520.6 8.4 psum.96
  529.1 0.6 multiply_reduce_fusion.3
  529.7 126.3 %psum.97 = f32[]{:T(128)} all-reduce(f32[]{:T(128)} %multiply_reduce_fusion.3), channel_id=1, replica_groups=mesh['rows'=4,'cols'=64] {'cols'}, use_global_device_ids=true, to_apply=%region_12.13 | all-reduce | flops 1 | bytes 8 | tf_op jit(solution)/shard_map/psum | solution.py:88
  657.2 0.6 multiply_reduce_fusion.2
  657.8 124.6 %psum.98 = f32[]{:T(128)} all-reduce(f32[]{:T(128)} %get-tuple-element.8), channel_id=1, replica_groups=mesh['rows'=4,'cols'=64] {'cols'}, use_global_device_ids=true, to_apply=%region_14.15 | all-reduce | flops 1 | bytes 8 | tf_op jit(solution)/shard_map/psum | solution.py:27
  783.7 0.9 fusion.36
  784.8 0.6 fusion.6
  785.5 1.1 fusion.49
  786.6 2.0 reshape.192
  788.6 91.7 %all-gather.13.cloned.1.call-done = f32[64,1,65536]{2,1,0:T(1,128)} async-done(((f32[1,1,65536]{2,1,0:T(1,128)}), f32[64,1,65536]{2,1,0:T(1,128)}) %all-gather.13.cloned.1.call-update) | async-done | bytes 16777232 | tf_op jit(solution)/shard_map/all_gather | solution.py:85
  880.3 12.0 reduce_sum.115
  892.3 1.0 multiply_convert_fusion.1
  893.3 0.7 reshape.183
  894.0 1.1 fusion.25
  895.8 0.7 convolution_bitcast_fusion.1
  896.5 8.4 psum.99
  905.0 0.7 multiply_reduce_fusion.1
  905.6 126.2 %psum.100 = f32[]{:T(128)} all-reduce(f32[]{:T(128)} %multiply_reduce_fusion.1), channel_id=1, replica_groups=mesh['rows'=4,'cols'=64] {'cols'}, use_global_device_ids=true, to_apply=%region_18.19 | all-reduce | flops 1 | bytes 8 | tf_op jit(solution)/shard_map/psum | solution.py:88
  1033.2 0.6 multiply_reduce_fusion
  1033.8 124.7 %psum.101 = f32[]{:T(128)} all-reduce(f32[]{:T(128)} %multiply_reduce_fusion), channel_id=1, replica_groups=mesh['rows'=4,'cols'=64] {'cols'}, use_global_device_ids=true, to_apply=%region_20.21 | all-reduce | flops 1 | bytes 8 | tf_op jit(solution)/shard_map/psum | solution.py:27
  1159.7 0.9 fusion.33
  1160.8 0.6 fusion.2
  1161.5 1.1 fusion.46
  1162.6 2.0 reshape.194
  1164.6 91.8 %all-gather.15.cloned.1.call-done = f32[64,1,65536]{2,1,0:T(1,128)} async-done(((f32[1,1,65536]{2,1,0:T(1,128)}), f32[64,1,65536]{2,1,0:T(1,128)}) %all-gather.15.cloned.1.call-update) | async-done | bytes 16777232 | tf_op jit(solution)/shard_map/all_gather | solution.py:85
  1256.3 12.0 reduce_sum.118
  1268.4 1.0 multiply_convert_fusion
  1269.5 0.8 fusion.26
  1271.0 0.7 convolution_bitcast_fusion
  1271.7 8.4 psum.102
  1280.1 0.6 fusion.76
  1280.7 126.3 %psum.103 = f32[]{:T(128)} all-reduce(f32[]{:T(128)} %fusion.76), channel_id=1, replica_groups=mesh['rows'=4,'cols'=64] {'cols'}, use_global_device_ids=true, to_apply=%region_24.25 | all-reduce | flops 1 | bytes 8 | tf_op jit(solution)/shard_map/psum | solution.py:88
  1408.3 1.4 dynamic-slice_subtract_fusion
  (90 shorter events, 4.8 us)
Async XLA Ops:
  7.2 2.6 copy-start
  7.2 2.9 copy-start.18
  7.2 2.9 copy-start.13
  7.2 120.0 %all-gather.9.cloned.1.call-start = ((), (), s32[]{:S(2)}) async-start(), calls=%async_computation | async-start | bytes 17039360 | tf_op jit(solution)/shard_map/all_gather | solution.py:85
  9.7 11.3 copy-start.2
  9.7 11.3 copy-start.8
  10.8 12.1 copy-start.10
  24.2 114.9 %copy-start.1 = (f32[65536]{0:T(1024)S(1)}, f32[65536]{0:T(1024)}, u32[]{:S(2)}) copy-start(f32[65536]{0:T(1024)} %param.13) | copy-start | bytes 786436
  24.3 479.6 %all-gather.11.cloned.1.call-start = ((), (), s32[]{:S(2)}) async-start(), calls=%async_computation.1 | async-start | bytes 17039360 | tf_op jit(solution)/shard_map/all_gather | solution.py:85
  142.0 266.2 %copy-start.14 = (s32[1,4]{1,0:T(1,128)S(1)}, s32[1,4]{1,0:T(1,128)}, u32[]{:S(2)}) copy-start(s32[1,4]{1,0:T(1,128)} %param.11) | copy-start | bytes 52
  142.0 266.2 %copy-start.19 = (s32[1,4]{1,0:T(1,128)S(1)}, s32[1,4]{1,0:T(1,128)}, u32[]{:S(2)}) copy-start(s32[1,4]{1,0:T(1,128)} %param.10) | copy-start | bytes 52
  412.1 468.3 %all-gather.13.cloned.1.call-start = ((), (), s32[]{:S(2)}) async-start(), calls=%async_computation.2 | async-start | bytes 17039360 | tf_op jit(solution)/shard_map/all_gather | solution.py:85
  518.6 266.0 %copy-start.15 = (s32[1,4]{1,0:T(1,128)S(1)}, s32[1,4]{1,0:T(1,128)}, u32[]{:S(2)}) copy-start(s32[1,4]{1,0:T(1,128)} %param.11) | copy-start | bytes 52
  518.6 266.0 %copy-start.20 = (s32[1,4]{1,0:T(1,128)S(1)}, s32[1,4]{1,0:T(1,128)}, u32[]{:S(2)}) copy-start(s32[1,4]{1,0:T(1,128)} %param.10) | copy-start | bytes 52
  520.0 265.5 %copy-start.11 = (s32[1,4]{1,0:T(1,128)S(1)}, s32[1,4]{1,0:T(1,128)}, u32[]{:S(2)}) copy-start(s32[1,4]{1,0:T(1,128)} %param.9) | copy-start | bytes 52
  657.8 130.7 %copy-start.3 = (f32[1024]{0:T(1024)}, f32[1024]{0:T(1024)S(1)}, u32[]{:S(2)}) copy-start(f32[1024]{0:T(1024)S(1)} %get-tuple-element.9) | copy-start | bytes 12292
  788.6 467.8 %all-gather.15.cloned.1.call-start = ((), (), s32[]{:S(2)}) async-start(), calls=%async_computation.3 | async-start | bytes 17039360 | tf_op jit(solution)/shard_map/all_gather | solution.py:85
  894.0 1.5 copy-start.16
  894.0 1.5 copy-start.21
  894.0 139.1 %copy-start.4 = (f32[1024]{0:T(1024)S(1)}, f32[1024]{0:T(1024)}, u32[]{:S(2)}) copy-start(f32[1024]{0:T(1024)} %copy-done.3) | copy-start | bytes 12292
  895.8 265.6 %copy-start.12 = (s32[1,4]{1,0:T(1,128)S(1)}, s32[1,4]{1,0:T(1,128)}, u32[]{:S(2)}) copy-start(s32[1,4]{1,0:T(1,128)} %param.9) | copy-start | bytes 52
  905.0 259.6 %copy-start.6 = (f32[1024]{0:T(1024)}, f32[1024]{0:T(1024)S(1)}, u32[]{:S(2)}) copy-start(f32[1024]{0:T(1024)S(1)} %psum.99) | copy-start | bytes 12292
  1269.3 1.4 copy-start.17
  1269.4 1.4 copy-start.22
  1269.4 10.7 copy-start.5
  1269.4 10.7 copy-start.7
  1269.4 138.9 %copy-start.9 = (f32[1024]{0:T(1024)S(1)}, f32[1024]{0:T(1024)}, u32[]{:S(2)}) copy-start(f32[1024]{0:T(1024)} %param.15) | copy-start | bytes 12292
Sparse Core Ops, SparseCore 0:
  24.4 102.7 all-gather.8
  412.2 91.6 all-gather.10
  788.7 91.6 all-gather.12
  1164.7 91.6 all-gather.14
